TPU v7x, 32 devices: a whole 2x2x4 slice. The times are simulated.
32 devices in a mesh: dp: 4 (over y, core), mp: 8 (over z, x).
Axes of the slice: x: 2, y: 2, z: 4, core: 2. Of those that a mesh axis runs over, the one named last changes fastest.
Arguments:
- activations: bfloat16 [1024, 8192], P('dp', 'mp'), may hold values from -40 to 40
- out_grads: bfloat16 [1024, 8192], P('dp', 'mp'), may hold values from -40 to 40
- basis_in: bfloat16 [8192, 8192], P(None, 'mp'), may hold values from -1 to 1
- basis_out: bfloat16 [8192, 8192], P(None, 'mp'), may hold values from -1 to 1
- grad_eigen: bfloat16 [8192, 8192], P('mp', 'dp'), may hold values from -8 to 8
Outputs:
- precond: bfloat16 [8192, 8192], P(('mp', 'dp'))
All inputs are finite; a program needn't handle non-finite values.
Results may differ from a plain program's by a relative error of at most 0.015.
Values may be sent and summed in bfloat16 or wider, within the bound.
A program may use at most 128 MiB of HBM per device.

v0:
```python
import jax
import jax.numpy as jnp
from jax import lax
from jax.sharding import PartitionSpec as P

damping = 0.1


def projector(basis, piece):
    return jnp.dot(piece, basis, preferred_element_type=jnp.float32)


def per_device(activations, out_grads, basis_in, basis_out, grad_eigen):
    tok_rows = activations.shape[0]
    groups = lax.axis_size("dp")
    proj_in = projector(basis_in, lax.all_gather(activations, "mp", axis=1, tiled=True))
    proj_out = projector(basis_out, lax.all_gather(out_grads, "mp", axis=1, tiled=True))
    squares_in = (proj_in * proj_in).astype(jnp.bfloat16)
    squares_out = (proj_out * proj_out).astype(jnp.bfloat16)
    partial_sums = lax.dot_general(
        squares_in,
        lax.all_gather(squares_out, "mp", axis=1, tiled=True),
        (((0,), (0,)), ((), ())),
        preferred_element_type=jnp.float32,
    )
    summed = lax.psum_scatter(
        partial_sums.astype(jnp.bfloat16), "dp", scatter_dimension=1, tiled=True
    ).astype(jnp.float32)
    scaling = summed / (tok_rows * groups)
    block_result = (grad_eigen.astype(jnp.float32) / (scaling + damping)).astype(jnp.bfloat16)
    return lax.all_to_all(block_result, "dp", split_axis=0, concat_axis=1, tiled=True)


def solution(mesh):
    placed = (P("dp", "mp"), P("dp", "mp"), P(None, "mp"), P(None, "mp"), P("mp", "dp"))
    return jax.shard_map(
        per_device, mesh=mesh, in_specs=placed, out_specs=P(("mp", "dp"), None), check_vma=False
    )
```

profile of v0, /device:TPU:0, one launch (start us, length us, event | category | flops | bytes accessed | tf_op | source)
XLA Modules:
  0.0 450.2 jit_solution(10755244098063213421)
XLA Ops:
  6.5 0.0 all-gather.6.cloned.1.call-start
  6.5 0.7 all-gather.6.cloned.1.call-update
  7.3 0.0 all-gather.4.cloned.1.call-start
  7.3 0.7 all-gather.4.cloned.1.call-update
  8.0 0.0 all-gather.8.cloned.1.call-start
  8.1 77.6 %all-gather.6.cloned.1.call-done = bf16[256,8192]{1,0:T(8,128)(2,1)} async-done(((bf16[256,1024]{1,0:T(8,128)(2,1)}), bf16[256,8192]{1,0:T(8,128)(2,1)}) %all-gather.6.cloned.1.call-update) | async-done | bytes 4194320 | tf_op jit(solution)/shard_map/all_gather | solution.py:17
  85.6 12.3 %fusion.1 = bf16[256,1024]{1,0:T(8,128)(2,1)} fusion(bf16[256,8192]{1,0:T(8,128)(2,1)} %all-gather.6.cloned.1.call-done, bf16[8192,1024]{1,0:T(8,128)(2,1)} %param.8), kind=kOutput, calls=%fused_computation.5 | convolution fusion | flops 4295491584 | bytes 21495808 | tf_op jit(solution)/shard_map/dot_general | solution.py:10
  98.0 0.0 all-gather.8.cloned.1.call-update
  98.0 0.0 reduce-scatter.2.cloned.1.call-start
  98.0 61.5 %all-gather.4.cloned.1.call-done = bf16[256,8192]{1,0:T(8,128)(2,1)} async-done(((bf16[256,1024]{1,0:T(8,128)(2,1)}), bf16[256,8192]{1,0:T(8,128)(2,1)}) %all-gather.4.cloned.1.call-update) | async-done | bytes 4194320 | tf_op jit(solution)/shard_map/all_gather | solution.py:16
  159.5 73.9 %all-gather.8.cloned.1.call-done = bf16[256,8192]{1,0:T(8,128)(2,1)} async-done(((bf16[256,1024]{1,0:T(8,128)(2,1)}), bf16[256,8192]{1,0:T(8,128)(2,1)}) %all-gather.8.cloned.1.call-update) | async-done | bytes 4194320 | tf_op jit(solution)/shard_map/all_gather | solution.py:22
  233.4 28.2 %convolution_convert_fusion = bf16[1024,8192]{1,0:T(8,128)(2,1)} fusion(bf16[256,8192]{1,0:T(8,128)(2,1)} %all-gather.8.cloned.1.call-done, bf16[256,8192]{1,0:T(8,128)(2,1)} %all-gather.4.cloned.1.call-done, bf16[8192,1024]{1,0:T(8,128)(2,1)} %param.7), kind=kOutput, calls=%fused_computation | convolution fusion | flops 8598847488 | bytes 41943040 | tf_op jit(solution)/shard_map/dot_general | solution.py:20
  261.6 0.0 reduce-scatter.2.cloned.1.call-update
  261.7 124.5 %reduce-scatter.2.cloned.1.call-done = bf16[1024,2048]{1,0:T(8,128)(2,1)} async-done(((bf16[1024,8192]{1,0:T(8,128)(2,1)}), bf16[1024,2048]{1,0:T(8,128)(2,1)}) %reduce-scatter.2.cloned.1.call-update) | async-done | bytes 4194320 | tf_op jit(solution)/shard_map/reduce_scatter | solution.py:26
  386.2 4.4 divide_convert_fusion
  390.6 50.7 %all_to_all.19 = bf16[4,256,2048]{2,1,0:T(8,128)(2,1)S(1)} all-to-all(bf16[4,256,2048]{2,1,0:T(8,128)(2,1)S(1)} %bitcast.9), channel_id=1, replica_groups=mesh['dp'=4,'mp'=8] {'dp'}, dimensions={0} | all-to-all | bytes 8388608 | tf_op jit(solution)/shard_map/all_to_all | solution.py:31
  441.4 2.3 copy.7
Async XLA Ops:
  6.5 79.1 %all-gather.6.cloned.1.call-start = ((), (), s32[]{:S(2)}) async-start(), calls=%async_computation.3 | async-start | bytes 4718592 | tf_op jit(solution)/shard_map/all_gather | solution.py:17
  7.3 152.3 %all-gather.4.cloned.1.call-start = ((), (), s32[]{:S(2)}) async-start(), calls=%async_computation.2 | async-start | bytes 4718592 | tf_op jit(solution)/shard_map/all_gather | solution.py:16
  8.0 225.4 %all-gather.8.cloned.1.call-start = ((), (), s32[]{:S(2)}) async-start(), calls=%async_computation.4 | async-start | bytes 4718592 | tf_op jit(solution)/shard_map/all_gather | solution.py:22
  98.0 288.2 %reduce-scatter.2.cloned.1.call-start = ((), (), s32[]{:S(2)}) async-start(), calls=%async_computation.5 | async-start | bytes 20971520 | tf_op jit(solution)/shard_map/reduce_scatter | solution.py:26
Sparse Core Ops, SparseCore 0:
  9.5 76.0 all-gather.5
  87.8 71.6 all-gather.3
  161.7 71.6 all-gather.7
  261.8 124.3 reduce-scatter.1
where the time goes:
time: 450 us
  waiting for transfers between devices  339 us (75%)
  blocking collectives  50.7 us (11%)
  matrix products  40.6 us (9%)
  between operations  13.1 us (3%)
    reduce_scatter x1, waiting for transfers between devices, per_device(): lax.psum_scatter(partial_sums.astype(jnp.bfloat16), 'dp', scatter_dimensi...  125 us
    all_gather x1, waiting for transfers between devices, per_device(): lax.all_gather(out_grads, 'mp', axis=1, tiled=True)  77.6 us
    all_gather x1, waiting for transfers between devices, per_device(): lax.all_gather(squares_out, 'mp', axis=1, tiled=True)  73.9 us
    all_gather x1, waiting for transfers between devices, per_device(): lax.all_gather(activations, 'mp', axis=1, tiled=True)  61.5 us
    all_to_all x1, blocking collectives, per_device(): lax.all_to_all(block_result, 'dp', split_axis=0, concat_axis=1, tiled=True)  50.7 us
    dot_general x1, matrix products, per_device(): lax.dot_general(squares_in, lax.all_gather(squares_out, 'mp', axis=1, til...  28.2 us
    dot_general x1, matrix products, projector(): return jnp.dot(piece, basis, preferred_element_type=jnp.float32)  12.3 us
  transfers between devices with their start and end apart: 4, of which 4 were waited for; matrix products, arithmetic and copies ran while one was open for 3% of the time, Pallas kernels for 0%

commit v1 on v0

--- a/solution.py
+++ b/solution.py
@@ -1,16 +1,23 @@
+import functools
+
 import jax
 import jax.numpy as jnp
 from jax import lax
+from jax.experimental import pallas as pl
+from jax.experimental.pallas import tpu as pltpu
 from jax.sharding import PartitionSpec as P
 
 damping = 0.1
+MESH = pl.DeviceIdType.MESH
+OUT, IN, SQ = 0, 1, 2
+UP, DOWN = 0, 1
 
 
 def projector(basis, piece):
     return jnp.dot(piece, basis, preferred_element_type=jnp.float32)
 
 
-def per_device(activations, out_grads, basis_in, basis_out, grad_eigen):
+def general(activations, out_grads, basis_in, basis_out, grad_eigen):
     tok_rows = activations.shape[0]
     groups = lax.axis_size("dp")
     proj_in = projector(basis_in, lax.all_gather(activations, "mp", axis=1, tiled=True))
@@ -31,8 +38,320 @@
     return lax.all_to_all(block_result, "dp", split_axis=0, concat_axis=1, tiled=True)
 
 
+def kernel(
+    act, og, basis_in, basis_out, grad, out,
+    held, squares, sq_in, sq_in_send, grads, basis, acc,
+    load_sem, zsend, zrecv, xsend, xrecv, ysend, yrecv, csend, crecv, ysend2, gsend, grecv, isend, irecv,
+):
+    tok, feat = act.shape
+    n_mp, n_dp = held.shape[1], squares.shape[0]
+    n_z = n_mp // 2
+    rows = out.shape[0]
+    width = grad.shape[1]
+    d, m = lax.axis_index("dp"), lax.axis_index("mp")
+    y, c = d // 2, d % 2
+    z, x = m // 2, m % 2
+    y_peer, c_peer, x_peer = (1 - y) * 2 + c, y * 2 + 1 - c, z * 2 + 1 - x
+    others = [(d + i) % n_dp for i in range(1, n_dp)]
+
+    def slot_of(step, way, other_x=False):
+        at = z - step if way == UP else z + step
+        return at * 2 + ((1 - x) if other_x else x)
+
+    def there(step, way):
+        return z >= step if way == UP else z + step < n_z
+
+    def ways(step):
+        return (UP,) if step == 0 else (UP, DOWN)
+
+    def buffer(a, slot, owner=None):
+        if a == SQ:
+            return squares.at[d if owner is None else owner, slot]
+        return held.at[a, slot]
+
+    def copy(ref, send, recv, target):
+        return pltpu.make_async_remote_copy(
+            src_ref=ref, dst_ref=ref, send_sem=send, recv_sem=recv,
+            device_id=target, device_id_type=MESH,
+        )
+
+    def z_copy(a, step, way, slot):
+        target = m + 2 if way == UP else m - 2
+        return copy(buffer(a, slot), zsend.at[a, step, way], zrecv.at[a, step, way], {"mp": target})
+
+    def x_copy(a, step, way, slot):
+        return copy(buffer(a, slot), xsend.at[a, step, way], xrecv.at[a, step, way], {"mp": x_peer})
+
+    def y_copy(step, way, other_x, owner):
+        ref = buffer(SQ, slot_of(step, way, other_x), owner)
+        return copy(ref, ysend.at[step, way, other_x], yrecv.at[step, way, other_x], {"dp": y_peer})
+
+    def c_copy(step, way, other_x, far, owner):
+        ref = buffer(SQ, slot_of(step, way, other_x), owner)
+        return copy(ref, csend.at[step, way, other_x, far], crecv.at[step, way, other_x, far], {"dp": c_peer})
+
+    def can_pass(step, way):
+        return (z < n_z - 1) if way == UP else (z > 0)
+
+    def send_z(a, step, way):
+        @pl.when(can_pass(step, way))
+        def _():
+            z_copy(a, step, way, slot_of(step, way)).start()
+
+    def spread(step, way, other_x):
+        y_copy(step, way, other_x, d).start()
+        c_copy(step, way, other_x, 0, d).start()
+
+    def first(a):
+        send_z(a, 0, UP)
+        send_z(a, 0, DOWN)
+        x_copy(a, 0, UP, m).start()
+        if a == SQ:
+            spread(0, UP, 0)
+
+    def pass_on(a, step):
+        for way in ways(step):
+            @pl.when(there(step, way))
+            def _():
+                z_copy(a, step - 1, way, slot_of(step, way)).wait_recv()
+                if step < n_z - 1:
+                    send_z(a, step, way)
+                x_copy(a, step, way, slot_of(step, way)).start()
+                if a == SQ:
+                    spread(step, way, 0)
+
+    def from_x(a, step):
+        for way in ways(step):
+            @pl.when(there(step, way))
+            def _():
+                x_copy(a, step, way, slot_of(step, way, True)).wait_recv()
+                if a == SQ:
+                    spread(step, way, 1)
+
+    def from_y(step):
+        for way in ways(step):
+            @pl.when(there(step, way))
+            def _():
+                for other_x in (0, 1):
+                    y_copy(step, way, other_x, y_peer).wait_recv()
+                    c_copy(step, way, other_x, 1, y_peer).start()
+
+    def load_basis(source):
+        return [
+            pltpu.make_async_copy(source.at[pl.ds(i * feat, feat), :], basis.at[i], load_sem.at[i])
+            for i in range(n_mp)
+        ]
+
+    def multiply(a, near):
+        tile = 256
+
+        def one(i, carry):
+            far = jnp.abs(i // 2 - z)
+            wanted = far <= 1 if near else far > 1
+
+            @pl.when(wanted)
+            def _():
+                @pl.loop(0, acc.shape[1] // tile)
+                def _(j):
+                    cols = pl.ds(pl.multiple_of(j * tile, tile), tile)
+                    acc[:, cols] += jnp.dot(
+                        held[a, i], basis[i, :, cols], preferred_element_type=jnp.float32
+                    )
+            return carry
+
+        lax.fori_loop(0, n_mp, one, 0)
+
+    own_out = pltpu.make_async_copy(og, held.at[OUT, m], load_sem.at[n_mp])
+    own_in = pltpu.make_async_copy(act, held.at[IN, m], load_sem.at[n_mp + 1])
+    own_grad = pltpu.make_async_copy(
+        grad.at[pl.ds(pl.multiple_of(d * rows, rows), rows), :], grads.at[d], load_sem.at[n_mp + 2]
+    )
+    own_out.start()
+    own_in.start()
+    own_grad.start()
+    for one in load_basis(basis_out):
+        one.start()
+
+    barrier = pltpu.get_barrier_semaphore()
+    peers = [{"mp": x_peer}] + [{"dp": other} for other in others]
+    for peer in peers:
+        pl.semaphore_signal(barrier, inc=1, device_id=peer, device_id_type=MESH)
+
+    @pl.when(z > 0)
+    def _():
+        pl.semaphore_signal(barrier, inc=1, device_id={"mp": m - 2}, device_id_type=MESH)
+
+    @pl.when(z < n_z - 1)
+    def _():
+        pl.semaphore_signal(barrier, inc=1, device_id={"mp": m + 2}, device_id_type=MESH)
+
+    inner = (z > 0).astype(jnp.int32) + (z < n_z - 1).astype(jnp.int32)
+    pl.semaphore_wait(barrier, len(peers) + inner)
+
+    def grad_copy(k, other):
+        return pltpu.make_async_remote_copy(
+            src_ref=grad.at[pl.ds(pl.multiple_of(other * rows, rows), rows), :], dst_ref=grads.at[d],
+            send_sem=gsend.at[k], recv_sem=grecv.at[k],
+            device_id={"dp": other}, device_id_type=MESH,
+        )
+
+    def in_copy(k, other):
+        return pltpu.make_async_remote_copy(
+            src_ref=sq_in_send.at[other], dst_ref=sq_in.at[d],
+            send_sem=isend.at[k], recv_sem=irecv.at[k],
+            device_id={"dp": other}, device_id_type=MESH,
+        )
+
+    own_out.wait()
+    first(OUT)
+    for k, other in enumerate(others):
+        grad_copy(k, other).start()
+    own_in.wait()
+    for step in range(1, n_z):
+        pass_on(OUT, step)
+    first(IN)
+
+    acc[...] = jnp.zeros_like(acc)
+    for one in load_basis(basis_out):
+        one.wait()
+    for step in (0, 1):
+        from_x(OUT, step)
+    multiply(OUT, True)
+    for step in range(2, n_z):
+        from_x(OUT, step)
+    multiply(OUT, False)
+    squares[d, m] = (acc[...] * acc[...]).astype(jnp.bfloat16)
+    first(SQ)
+    for one in load_basis(basis_in):
+        one.start()
+    acc[...] = jnp.zeros_like(acc)
+
+    for step in range(1, n_z):
+        from_x(SQ, step - 1)
+        pass_on(SQ, step)
+        pass_on(IN, step)
+        if step > 1:
+            from_y(step - 2)
+    from_x(SQ, n_z - 1)
+
+    for one in load_basis(basis_in):
+        one.wait()
+    for step in (0, 1):
+        from_x(IN, step)
+    multiply(IN, True)
+    for step in range(2, n_z):
+        from_x(IN, step)
+    multiply(IN, False)
+    for k in range(n_dp):
+        part = acc[:, k * rows:(k + 1) * rows]
+        sq_in_send[k] = (part * part).T.astype(jnp.bfloat16)
+    for k, other in enumerate(others):
+        in_copy(k, other).start()
+    sq_in[d] = sq_in_send[d]
+
+    for step in range(n_z - 2, n_z):
+        from_y(step)
+
+    own_grad.wait()
+    for k, other in enumerate(others):
+        back = (d + n_dp - k - 1) % n_dp
+        pltpu.make_async_remote_copy(
+            src_ref=grads.at[back], dst_ref=grads.at[back], send_sem=gsend.at[k], recv_sem=grecv.at[k],
+            device_id={"dp": other}, device_id_type=MESH,
+        ).wait_recv()
+        pltpu.make_async_remote_copy(
+            src_ref=sq_in.at[back], dst_ref=sq_in.at[back], send_sem=isend.at[k], recv_sem=irecv.at[k],
+            device_id={"dp": other}, device_id_type=MESH,
+        ).wait_recv()
+    for step in range(n_z):
+        for way in ways(step):
+            @pl.when(there(step, way))
+            def _():
+                for other_x in (0, 1):
+                    c_copy(step, way, other_x, 0, c_peer).wait_recv()
+                    c_copy(step, way, other_x, 1, (1 - y) * 2 + 1 - c).wait_recv()
+
+    tile = 256
+    per_block, per_grad = feat // tile, width // tile
+
+    @pl.loop(0, out.shape[1] // tile)
+    def _(t):
+        block, cols = t // per_block, pl.ds(pl.multiple_of((t % per_block) * tile, tile), tile)
+        total = jnp.zeros((rows, tile), jnp.float32)
+        for k in range(n_dp):
+            total += jnp.dot(sq_in[k], squares[k, block, :, cols], preferred_element_type=jnp.float32)
+        scaling = total / (tok * n_dp)
+        cols_g = pl.ds(pl.multiple_of((t % per_grad) * tile, tile), tile)
+        top = grads[t // per_grad, :, cols_g].astype(jnp.float32)
+        out[:, pl.ds(pl.multiple_of(t * tile, tile), tile)] = (top / (scaling + damping)).astype(out.dtype)
+
+    for k, other in enumerate(others):
+        grad_copy(k, other).wait_send()
+        in_copy(k, other).wait_send()
+    for step in range(n_z):
+        for way in ways(step):
+            @pl.when(there(step, way))
+            def _():
+                for a in (OUT, IN, SQ):
+                    x_copy(a, step, way, slot_of(step, way)).wait_send()
+                for other_x in (0, 1):
+                    y_copy(step, way, other_x, d).wait_send()
+                    c_copy(step, way, other_x, 0, d).wait_send()
+                    c_copy(step, way, other_x, 1, y_peer).wait_send()
+        if step < n_z - 1:
+            for way in (UP, DOWN):
+                @pl.when(there(step, way) & can_pass(step, way))
+                def _():
+                    for a in (OUT, IN, SQ):
+                        z_copy(a, step, way, slot_of(step, way)).wait_send()
+
+
+def per_device(activations, out_grads, basis_in, basis_out, grad_eigen):
+    tok, feat = activations.shape
+    n_dp, n_mp = lax.axis_size("dp"), lax.axis_size("mp")
+    depth, cols = basis_in.shape
+    height, width = grad_eigen.shape
+    rows = height // n_dp
+    n_z = n_mp // 2
+    dma = pltpu.SemaphoreType.DMA
+    spec = pl.BlockSpec(memory_space=pl.ANY)
+    return pl.pallas_call(
+        kernel,
+        out_shape=jax.ShapeDtypeStruct((rows, depth), jnp.bfloat16),
+        in_specs=[spec] * 5,
+        out_specs=pl.BlockSpec(memory_space=pltpu.VMEM),
+        scratch_shapes=[
+            pltpu.VMEM((2, n_mp, tok, feat), jnp.bfloat16),
+            pltpu.VMEM((n_dp, n_mp, tok, cols), jnp.bfloat16),
+            pltpu.VMEM((n_dp, rows, tok), jnp.bfloat16),
+            pltpu.VMEM((n_dp, rows, tok), jnp.bfloat16),
+            pltpu.VMEM((n_dp, rows, width), jnp.bfloat16),
+            pltpu.VMEM((n_mp, feat, cols), jnp.bfloat16),
+            pltpu.VMEM((tok, cols), jnp.float32),
+            dma((n_mp + 3,)),
+            dma((3, n_z, 2)), dma((3, n_z, 2)),
+            dma((3, n_z, 2)), dma((3, n_z, 2)),
+            dma((n_z, 2, 2)), dma((n_z, 2, 2)),
+            dma((n_z, 2, 2, 2)), dma((n_z, 2, 2, 2)),
+            dma((n_dp,)),
+            dma((n_dp,)), dma((n_dp,)),
+            dma((n_dp,)), dma((n_dp,)),
+        ],
+        compiler_params=pltpu.CompilerParams(
+            collective_id=0, has_side_effects=True, vmem_limit_bytes=60 * 1024 * 1024
+        ),
+        cost_estimate=pl.CostEstimate(
+            flops=4 * tok * depth * cols + 2 * rows * tok * n_dp * depth,
+            bytes_accessed=4 * depth * cols + 4 * height * width,
+            transcendentals=0,
+        ),
+    )(activations, out_grads, basis_in, basis_out, grad_eigen)
+
+
 def solution(mesh):
     placed = (P("dp", "mp"), P("dp", "mp"), P(None, "mp"), P(None, "mp"), P("mp", "dp"))
+    routed = (mesh.shape["dp"], mesh.shape["mp"]) == (4, 8)
     return jax.shard_map(
-        per_device, mesh=mesh, in_specs=placed, out_specs=P(("mp", "dp"), None), check_vma=False
+        per_device if routed else general,
+        mesh=mesh, in_specs=placed, out_specs=P(("mp", "dp"), None), check_vma=False,
     )

time: 450 us -> 176 us (0.39)
  waiting for transfers between devices: 339 us -> 0 us
  Pallas kernels: 0 us -> 170 us
  blocking collectives: 50.7 us -> 0 us
  matrix products: 40.6 us -> 0 us
  between operations: 13.1 us -> 0.01 us
    all_gather x3 -> x0, waiting for transfers between devices: 213 us -> none  [the longest x1 77.6 us: per_device(): lax.all_gather(out_grads, 'mp', axis=1, tiled=True)]
    pallas_call x0 -> x1, Pallas kernels: none -> 170 us  [per_device(): pl.pallas_call(kernel, out_shape=jax.ShapeDtypeStruct((rows, depth), jnp....]
    reduce_scatter x1 -> x0, waiting for transfers between devices: 125 us -> none  [per_device(): lax.psum_scatter(partial_sums.astype(jnp.bfloat16), 'dp', scatter_dimensi...]
    all_to_all x1 -> x0, blocking collectives: 50.7 us -> none  [per_device(): lax.all_to_all(block_result, 'dp', split_axis=0, concat_axis=1, tiled=True)]
    dot_general x2 -> x0, matrix products: 40.6 us -> none  [the longest x1 28.2 us: per_device(): lax.dot_general(squares_in, lax.all_gather(squares_out, 'mp', axis=1, til...]
    unnamed x0 -> x1, local copies, waits for them, and re-layouts: none -> 4.64 us
  transfers between devices with their start and end apart: 4 -> 0, of which waited for: 4 -> 0; matrix products, arithmetic and copies ran while one was open for 3% -> 0% of each run, Pallas kernels for 0% -> 0%
where the time goes in v1:
time: 176 us; the launch traced here: 175 us
  Pallas kernels  170 us (97%)
  local copies, waits for them, and re-layouts  4.64 us (3%)
    pallas_call x1, Pallas kernels, per_device(): pl.pallas_call(kernel, out_shape=jax.ShapeDtypeStruct((rows, depth), jnp....  170 us
    unnamed x1, local copies, waits for them, and re-layouts  4.64 us

profile of v1, /device:TPU:0, one launch (start us, length us, event | category | flops | bytes accessed | tf_op | source)
XLA Modules:
  0.0 175.1 jit_solution(1332969112711503146)
XLA Ops:
  0.0 170.5 %shard_map.55 = bf16[256,8192]{1,0:T(8,128)(2,1)} custom-call(bf16[256,1024]{1,0:T(8,128)(2,1)} %act.1, bf16[256,1024]{1,0:T(8,128)(2,1)} %og.1, bf16[8192,1024]{1,0:T(8,128)(2,1)} %basis_in.1, bf16[8192,1024]{1,0:T(8,128)(2,1)} %basis_out.1, bf16[1024,2048]{1,0:T(8,128)(2,1)} %grad.1), custom_call_target="tpu_custom_call" | custom-call | flops 12884901888 | bytes 41943040 | tf_op jit(solution)/shard_map/pallas_call | solution.py:318
  170.5 4.6 %copy.7 = bf16[256,8192]{1,0:T(8,128)(2,1)} copy(bf16[256,8192]{1,0:T(8,128)(2,1)} %shard_map.55) | data formatting | bytes 8388608

commit v2 on v0

--- a/solution.py
+++ b/solution.py
@@ -1,16 +1,21 @@
 import jax
 import jax.numpy as jnp
 from jax import lax
+from jax.experimental import pallas as pl
+from jax.experimental.pallas import tpu as pltpu
 from jax.sharding import PartitionSpec as P
 
 damping = 0.1
+MESH = pl.DeviceIdType.MESH
+OUT, IN, SQ = 0, 1, 2
+UP, DOWN = 0, 1
 
 
 def projector(basis, piece):
     return jnp.dot(piece, basis, preferred_element_type=jnp.float32)
 
 
-def per_device(activations, out_grads, basis_in, basis_out, grad_eigen):
+def general(activations, out_grads, basis_in, basis_out, grad_eigen):
     tok_rows = activations.shape[0]
     groups = lax.axis_size("dp")
     proj_in = projector(basis_in, lax.all_gather(activations, "mp", axis=1, tiled=True))
@@ -31,8 +36,401 @@
     return lax.all_to_all(block_result, "dp", split_axis=0, concat_axis=1, tiled=True)
 
 
+def kernel(
+    act, og, basis_in, basis_out, grad, out,
+    held, squares, sq_in, sq_in_send, grads, basis, acc, result,
+    load_sem, store_sem, zsend, zrecv, xsend, xrecv, dsend, drecv, ysend, yrecv, csend, crecv,
+    gsend, grecv, isend, irecv,
+):
+    tok, feat = act.shape
+    n_mp, n_dp = held.shape[1], squares.shape[0]
+    n_z = n_mp // 2
+    rows = out.shape[0]
+    width = grad.shape[1]
+    half = tok // 2
+    d, m = lax.axis_index("dp"), lax.axis_index("mp")
+    y, c = d // 2, d % 2
+    z, x = m // 2, m % 2
+    y_peer, c_peer, x_peer = (1 - y) * 2 + c, y * 2 + 1 - c, z * 2 + 1 - x
+    diagonal = (1 - y) * 2 + 1 - c
+    others = [(d + i) % n_dp for i in range(1, n_dp)]
+    started = []
+
+    def do(wanted, action):
+        if wanted is True:
+            action()
+        else:
+            pl.when(wanted)(action)
+
+    def start(wanted, copy):
+        started.append((wanted, copy))
+        do(wanted, lambda: copy().start())
+
+    def arrived(wanted, copy):
+        do(wanted, lambda: copy().wait_recv())
+
+    def both(one, other):
+        if one is True:
+            return other
+        return one if other is True else one & other
+
+    def slot_of(step, way, other_x):
+        at = z - step if way == UP else z + step
+        return at * 2 + ((1 - x) if other_x else x)
+
+    def there(step, way):
+        if step == 0:
+            return True
+        return z >= step if way == UP else z + step < n_z
+
+    def ways(step):
+        return (UP,) if step == 0 else (UP, DOWN)
+
+    def can_pass(way):
+        return z < n_z - 1 if way == UP else z > 0
+
+    def paired(step, way, h):
+        if h == 0 or step == 0:
+            return False
+        return z == step if way == UP else z + step == n_z - 1
+
+    def alone(step, way, h):
+        if h == 0 or step == 0:
+            return there(step, way)
+        return z > step if way == UP else z + step < n_z - 1
+
+    def part(a, step, way, other_x, h, owner=None):
+        slot = slot_of(step, way, other_x)
+        lines = pl.ds(h * half, half)
+        if a == SQ:
+            return squares.at[d if owner is None else owner, slot, lines]
+        return held.at[a, slot, lines]
+
+    def remote(ref, send, recv, target):
+        return pltpu.make_async_remote_copy(
+            src_ref=ref, dst_ref=ref, send_sem=send, recv_sem=recv,
+            device_id=target, device_id_type=MESH,
+        )
+
+    def z_copy(a, step, way, other_x, h):
+        at = (a, step, way, other_x, h)
+        target = m + 2 if way == UP else m - 2
+        return remote(part(*at), zsend.at[at], zrecv.at[at], {"mp": target})
+
+    def x_copy(a, step, way, h, other_x=0):
+        at = (a, step, way, h)
+        return remote(part(a, step, way, other_x, h), xsend.at[at], xrecv.at[at], {"mp": x_peer})
+
+    def d_copy(h, other_x=0):
+        return remote(part(SQ, 0, UP, other_x, h, y_peer), dsend.at[h], drecv.at[h], {"mp": x_peer})
+
+    def y_copy(step, way, other_x, h, owner):
+        at = (step, way, other_x, h)
+        return remote(part(SQ, *at, owner), ysend.at[at], yrecv.at[at], {"dp": y_peer})
+
+    def c_copy(step, way, other_x, h, far, owner):
+        at = (step, way, other_x, h)
+        return remote(part(SQ, *at, owner), csend.at[(far,) + at], crecv.at[(far,) + at], {"dp": c_peer})
+
+    def send_z(a, step, way, other_x, h, wanted):
+        if step < n_z - 1:
+            start(both(wanted, can_pass(way)), lambda: z_copy(a, step, way, other_x, h))
+
+    def send_x(a, step):
+        for h in (0, 1):
+            for way in ways(step):
+                start(alone(step, way, h), lambda way=way, h=h: x_copy(a, step, way, h))
+
+    def spread(step, way, other_x, h, wanted):
+        if step > 0 or not other_x:
+            start(wanted, lambda: y_copy(step, way, other_x, h, d))
+        start(wanted, lambda: c_copy(step, way, other_x, h, 0, d))
+
+    def first_z(a):
+        for h in (0, 1):
+            for way in (UP, DOWN):
+                send_z(a, 0, way, 0, h, True)
+
+    def along_z(a, step):
+        for h in (0, 1):
+            for way in (UP, DOWN):
+                wanted = there(step, way)
+                arrived(wanted, lambda: z_copy_in(a, step, way, 0, h))
+                send_z(a, step, way, 0, h, wanted)
+                if a == SQ:
+                    spread(step, way, 0, h, wanted)
+
+    def z_copy_in(a, step, way, other_x, h):
+        ref = part(a, step, way, other_x, h)
+        at = (a, step - 1, way, other_x, h)
+        return remote(ref, zsend.at[at], zrecv.at[at], {"mp": x_peer})
+
+    def pairs(a, step):
+        for way in (UP, DOWN):
+            wanted = paired(step, way, 1)
+            arrived(wanted, lambda: z_copy_in(a, step, way, 1, 1))
+            send_z(a, step, way, 1, 1, wanted)
+            if a == SQ:
+                spread(step, way, 1, 1, wanted)
+
+    def from_x(a, step):
+        for h in (0, 1):
+            for way in ways(step):
+                wanted = alone(step, way, h)
+                arrived(wanted, lambda: x_copy(a, step, way, h, 1))
+                if step == 0 and h == 1:
+                    send_z(a, 0, UP, 1, h, z == 0)
+                    send_z(a, 0, DOWN, 1, h, z == n_z - 1)
+                if a == SQ:
+                    spread(step, way, 1, h, wanted)
+
+    def from_y(step):
+        for other_x in (0, 1) if step > 0 else (0,):
+            for h in (0, 1):
+                for way in ways(step):
+                    wanted = there(step, way)
+                    arrived(wanted, lambda: y_copy(step, way, other_x, h, y_peer))
+                    start(wanted, lambda way=way, other_x=other_x, h=h: c_copy(step, way, other_x, h, 1, y_peer))
+
+    def from_core(step):
+        for other_x in (0, 1):
+            for h in (0, 1):
+                for way in ways(step):
+                    wanted = there(step, way)
+                    arrived(wanted, lambda: c_copy(step, way, other_x, h, 0, c_peer))
+                    arrived(wanted, lambda: c_copy(step, way, other_x, h, 1, diagonal))
+
+    def load_basis(source):
+        return [
+            pltpu.make_async_copy(source.at[pl.ds(i * feat, feat), :], basis.at[i], load_sem.at[i])
+            for i in range(n_mp)
+        ]
+
+    tile = 256
+
+    def blocks_within(low, high, action):
+        def one(i, carry):
+            away = jnp.abs(i // 2 - z)
+            pl.when((away >= low) & (away <= high))(lambda: action(i))
+            return carry
+
+        lax.fori_loop(0, n_mp, one, 0)
+
+    def multiply(a, low, high):
+        def block(i):
+            @pl.loop(0, acc.shape[1] // tile)
+            def _(j):
+                cols = pl.ds(pl.multiple_of(j * tile, tile), tile)
+                acc[:, cols] += jnp.dot(held[a, i], basis[i, :, cols], preferred_element_type=jnp.float32)
+
+        blocks_within(low, high, block)
+
+    def store(i):
+        cols = pl.ds(pl.multiple_of(i * feat, feat), feat)
+        return pltpu.make_async_copy(result.at[:, cols], out.at[:, cols], store_sem.at[i])
+
+    def finish(low, high):
+        per_grad = width // feat
+
+        def block(i):
+            @pl.loop(0, feat // tile)
+            def _(j):
+                cols = pl.ds(pl.multiple_of(j * tile, tile), tile)
+                total = jnp.zeros((rows, tile), jnp.float32)
+                for k in range(n_dp):
+                    total += jnp.dot(sq_in[k], squares[k, i, :, cols], preferred_element_type=jnp.float32)
+                scaling = total / (tok * n_dp)
+                at_grad = pl.ds(pl.multiple_of((i % per_grad) * feat + j * tile, tile), tile)
+                top = grads[i // per_grad, :, at_grad].astype(jnp.float32)
+                at_out = pl.ds(pl.multiple_of(i * feat + j * tile, tile), tile)
+                result[:, at_out] = (top / (scaling + damping)).astype(result.dtype)
+
+            store(i).start()
+
+        blocks_within(low, high, block)
+
+    own_out = pltpu.make_async_copy(og, held.at[OUT, m], load_sem.at[n_mp])
+    own_in = pltpu.make_async_copy(act, held.at[IN, m], load_sem.at[n_mp + 1])
+    own_grad = pltpu.make_async_copy(
+        grad.at[pl.ds(pl.multiple_of(d * rows, rows), rows), :], grads.at[d], load_sem.at[n_mp + 2]
+    )
+    own_out.start()
+    own_in.start()
+    own_grad.start()
+    for one in load_basis(basis_out):
+        one.start()
+
+    barrier = pltpu.get_barrier_semaphore()
+    peers = [{"mp": x_peer}] + [{"dp": other} for other in others]
+    for peer in peers:
+        pl.semaphore_signal(barrier, inc=1, device_id=peer, device_id_type=MESH)
+    for way, target in ((UP, m + 2), (DOWN, m - 2)):
+        @pl.when(can_pass(way))
+        def _():
+            pl.semaphore_signal(barrier, inc=1, device_id={"mp": target}, device_id_type=MESH)
+
+    inner = (z > 0).astype(jnp.int32) + (z < n_z - 1).astype(jnp.int32)
+    pl.semaphore_wait(barrier, len(peers) + inner)
+
+    def grad_copy(k, other):
+        return pltpu.make_async_remote_copy(
+            src_ref=grad.at[pl.ds(pl.multiple_of(other * rows, rows), rows), :], dst_ref=grads.at[d],
+            send_sem=gsend.at[k], recv_sem=grecv.at[k],
+            device_id={"dp": other}, device_id_type=MESH,
+        )
+
+    def in_copy(k, other):
+        return pltpu.make_async_remote_copy(
+            src_ref=sq_in_send.at[other], dst_ref=sq_in.at[d],
+            send_sem=isend.at[k], recv_sem=irecv.at[k],
+            device_id={"dp": other}, device_id_type=MESH,
+        )
+
+    own_out.wait()
+    first_z(OUT)
+    send_x(OUT, 0)
+    for k, other in enumerate(others):
+        start(True, lambda k=k, other=other: grad_copy(k, other))
+    own_in.wait()
+    along_z(OUT, 1)
+    send_x(OUT, 1)
+    from_x(OUT, 0)
+    acc[...] = jnp.zeros_like(acc)
+    for one in load_basis(basis_out):
+        one.wait()
+    pairs(OUT, 1)
+    for step in range(2, n_z):
+        along_z(OUT, step)
+        send_x(OUT, step)
+        pairs(OUT, step)
+    first_z(IN)
+    from_x(OUT, 1)
+    multiply(OUT, 0, 1)
+    from_x(OUT, 2)
+    multiply(OUT, 2, 2)
+    for step in range(3, n_z):
+        from_x(OUT, step)
+    send_x(IN, 0)
+    multiply(OUT, 3, n_z)
+    squares[d, m] = (acc[...] * acc[...]).astype(jnp.bfloat16)
+
+    first_z(SQ)
+    send_x(SQ, 0)
+    for h in (0, 1):
+        spread(0, UP, 0, h, True)
+    for one in load_basis(basis_in):
+        one.start()
+    acc[...] = jnp.zeros_like(acc)
+
+    along_z(SQ, 1)
+    send_x(SQ, 1)
+    along_z(IN, 1)
+    from_x(IN, 0)
+    from_x(SQ, 0)
+    send_x(IN, 1)
+    for step in range(2, n_z):
+        along_z(SQ, step)
+        along_z(IN, step)
+        send_x(IN, step)
+        pairs(IN, step - 1)
+        pairs(SQ, step - 1)
+        if step == 2:
+            from_x(SQ, 1)
+            from_y(0)
+    for step in range(2, n_z):
+        send_x(SQ, step)
+        if step == 2:
+            for h in (0, 1):
+                start(True, lambda h=h: d_copy(h))
+    pairs(IN, n_z - 1)
+    pairs(SQ, n_z - 1)
+    for one in load_basis(basis_in):
+        one.wait()
+    from_x(IN, 1)
+    multiply(IN, 0, 1)
+    for step in range(2, n_z):
+        from_x(IN, step)
+    multiply(IN, 2, n_z)
+    for k in range(n_dp):
+        piece = acc[:, k * rows:(k + 1) * rows]
+        sq_in_send[k] = (piece * piece).T.astype(jnp.bfloat16)
+    for k, other in enumerate(others):
+        start(True, lambda k=k, other=other: in_copy(k, other))
+    sq_in[d] = sq_in_send[d]
+    from_x(SQ, 2)
+    from_y(1)
+    for h in (0, 1):
+        arrived(True, lambda: d_copy(h, 1))
+        start(True, lambda h=h: c_copy(0, UP, 1, h, 1, y_peer))
+    for step in range(3, n_z):
+        from_x(SQ, step)
+
+    own_grad.wait()
+    for k in range(n_dp - 1):
+        back = (d + n_dp - k - 1) % n_dp
+        remote(grads.at[back], gsend.at[k], grecv.at[k], {"dp": others[k]}).wait_recv()
+        remote(sq_in.at[back], isend.at[k], irecv.at[k], {"dp": others[k]}).wait_recv()
+    from_core(0)
+    from_core(1)
+    finish(0, 1)
+    for step in range(2, n_z):
+        from_y(step)
+        from_core(step)
+        finish(step, step)
+
+    for i in range(n_mp):
+        store(i).wait()
+    for wanted, copy in started:
+        do(wanted, lambda: copy().wait_send())
+
+
+def per_device(activations, out_grads, basis_in, basis_out, grad_eigen):
+    tok, feat = activations.shape
+    n_dp, n_mp = lax.axis_size("dp"), lax.axis_size("mp")
+    depth, cols = basis_in.shape
+    height, width = grad_eigen.shape
+    rows = height // n_dp
+    n_z = n_mp // 2
+    dma = pltpu.SemaphoreType.DMA
+    spec = pl.BlockSpec(memory_space=pl.ANY)
+    return pl.pallas_call(
+        kernel,
+        out_shape=jax.ShapeDtypeStruct((rows, depth), jnp.bfloat16),
+        in_specs=[spec] * 5,
+        out_specs=spec,
+        scratch_shapes=[
+            pltpu.VMEM((2, n_mp, tok, feat), jnp.bfloat16),
+            pltpu.VMEM((n_dp, n_mp, tok, cols), jnp.bfloat16),
+            pltpu.VMEM((n_dp, rows, tok), jnp.bfloat16),
+            pltpu.VMEM((n_dp, rows, tok), jnp.bfloat16),
+            pltpu.VMEM((n_dp, rows, width), jnp.bfloat16),
+            pltpu.VMEM((n_mp, feat, cols), jnp.bfloat16),
+            pltpu.VMEM((tok, cols), jnp.float32),
+            pltpu.VMEM((rows, depth), jnp.bfloat16),
+            dma((n_mp + 3,)), dma((n_mp,)),
+            dma((3, n_z - 1, 2, 2, 2)), dma((3, n_z - 1, 2, 2, 2)),
+            dma((3, n_z, 2, 2)), dma((3, n_z, 2, 2)),
+            dma((2,)), dma((2,)),
+            dma((n_z, 2, 2, 2)), dma((n_z, 2, 2, 2)),
+            dma((2, n_z, 2, 2, 2)), dma((2, n_z, 2, 2, 2)),
+            dma((n_dp,)), dma((n_dp,)),
+            dma((n_dp,)), dma((n_dp,)),
+        ],
+        compiler_params=pltpu.CompilerParams(
+            collective_id=0, has_side_effects=True, vmem_limit_bytes=60 * 1024 * 1024
+        ),
+        cost_estimate=pl.CostEstimate(
+            flops=4 * tok * depth * cols + 2 * rows * tok * n_dp * depth,
+            bytes_accessed=4 * depth * cols + 4 * height * width,
+            transcendentals=0,
+        ),
+    )(activations, out_grads, basis_in, basis_out, grad_eigen)
+
+
 def solution(mesh):
     placed = (P("dp", "mp"), P("dp", "mp"), P(None, "mp"), P(None, "mp"), P("mp", "dp"))
+    routed = (mesh.shape["dp"], mesh.shape["mp"]) == (4, 8)
     return jax.shard_map(
-        per_device, mesh=mesh, in_specs=placed, out_specs=P(("mp", "dp"), None), check_vma=False
+        per_device if routed else general,
+        mesh=mesh, in_specs=placed, out_specs=P(("mp", "dp"), None), check_vma=False,
     )

time: 450 us -> 174 us (0.39)
  waiting for transfers between devices: 339 us -> 0 us
  Pallas kernels: 0 us -> 169 us
  blocking collectives: 50.7 us -> 0 us
  matrix products: 40.6 us -> 0 us
  between operations: 13.1 us -> 0.01 us
    all_gather x3 -> x0, waiting for transfers between devices: 213 us -> none  [the longest x1 77.6 us: per_device(): lax.all_gather(out_grads, 'mp', axis=1, tiled=True)]
    pallas_call x0 -> x1, Pallas kernels: none -> 169 us  [per_device(): pl.pallas_call(kernel, out_shape=jax.ShapeDtypeStruct((rows, depth), jnp....]
    reduce_scatter x1 -> x0, waiting for transfers between devices: 125 us -> none  [per_device(): lax.psum_scatter(partial_sums.astype(jnp.bfloat16), 'dp', scatter_dimensi...]
    all_to_all x1 -> x0, blocking collectives: 50.7 us -> none  [per_device(): lax.all_to_all(block_result, 'dp', split_axis=0, concat_axis=1, tiled=True)]
    dot_general x2 -> x0, matrix products: 40.6 us -> none  [the longest x1 28.2 us: per_device(): lax.dot_general(squares_in, lax.all_gather(squares_out, 'mp', axis=1, til...]
    unnamed x0 -> x1, local copies, waits for them, and re-layouts: none -> 4.64 us
  transfers between devices with their start and end apart: 4 -> 0, of which waited for: 4 -> 0; matrix products, arithmetic and copies ran while one was open for 3% -> 0% of each run, Pallas kernels for 0% -> 0%
where the time goes in v2:
time: 174 us; the launch traced here: 173 us
  Pallas kernels  169 us (97%)
  local copies, waits for them, and re-layouts  4.64 us (3%)
    pallas_call x1, Pallas kernels, per_device(): pl.pallas_call(kernel, out_shape=jax.ShapeDtypeStruct((rows, depth), jnp....  169 us
    unnamed x1, local copies, waits for them, and re-layouts  4.64 us

profile of v2, /device:TPU:0, one launch (start us, length us, event | category | flops | bytes accessed | tf_op | source)
XLA Modules:
  0.0 173.4 jit_solution(9586102742028503164)
XLA Ops:
  0.0 168.8 %shard_map.55 = bf16[256,8192]{1,0:T(8,128)(2,1)} custom-call(bf16[256,1024]{1,0:T(8,128)(2,1)} %act.1, bf16[256,1024]{1,0:T(8,128)(2,1)} %og.1, bf16[8192,1024]{1,0:T(8,128)(2,1)} %basis_in.1, bf16[8192,1024]{1,0:T(8,128)(2,1)} %basis_out.1, bf16[1024,2048]{1,0:T(8,128)(2,1)} %grad.1), custom_call_target="tpu_custom_call" | custom-call | flops 12884901888 | bytes 41943040 | tf_op jit(solution)/shard_map/pallas_call | solution.py:396
  168.8 4.6 %copy.7 = bf16[256,8192]{1,0:T(8,128)(2,1)} copy(bf16[256,8192]{1,0:T(8,128)(2,1)} %shard_map.55) | data formatting | bytes 8388608

commit v3 on v2

--- a/solution.py
+++ b/solution.py
@@ -38,12 +38,12 @@
 
 def kernel(
     act, og, basis_in, basis_out, grad, out,
-    held, squares, sq_in, sq_in_send, grads, basis, acc, result,
+    held, squares, sq_in, sq_in_send, sq_all, grads, basis, acc, result,
     load_sem, store_sem, zsend, zrecv, xsend, xrecv, dsend, drecv, ysend, yrecv, csend, crecv,
     gsend, grecv, isend, irecv,
 ):
     tok, feat = act.shape
-    n_mp, n_dp = held.shape[1], squares.shape[0]
+    n_mp, n_dp = held.shape[1], sq_in.shape[0]
     n_z = n_mp // 2
     rows = out.shape[0]
     width = grad.shape[1]
@@ -101,10 +101,10 @@
 
     def part(a, step, way, other_x, h, owner=None):
         slot = slot_of(step, way, other_x)
-        lines = pl.ds(h * half, half)
         if a == SQ:
-            return squares.at[d if owner is None else owner, slot, lines]
-        return held.at[a, slot, lines]
+            lines = (d if owner is None else owner) * tok + h * half
+            return squares.at[slot, pl.ds(pl.multiple_of(lines, half), half)]
+        return held.at[a, slot, pl.ds(h * half, half)]
 
     def remote(ref, send, recv, target):
         return pltpu.make_async_remote_copy(
@@ -236,9 +236,7 @@
             @pl.loop(0, feat // tile)
             def _(j):
                 cols = pl.ds(pl.multiple_of(j * tile, tile), tile)
-                total = jnp.zeros((rows, tile), jnp.float32)
-                for k in range(n_dp):
-                    total += jnp.dot(sq_in[k], squares[k, i, :, cols], preferred_element_type=jnp.float32)
+                total = jnp.dot(sq_all[...], squares[i, :, cols], preferred_element_type=jnp.float32)
                 scaling = total / (tok * n_dp)
                 at_grad = pl.ds(pl.multiple_of((i % per_grad) * feat + j * tile, tile), tile)
                 top = grads[i // per_grad, :, at_grad].astype(jnp.float32)
@@ -299,20 +297,21 @@
     for one in load_basis(basis_out):
         one.wait()
     pairs(OUT, 1)
+    multiply(OUT, 0, 0)
     for step in range(2, n_z):
         along_z(OUT, step)
         send_x(OUT, step)
         pairs(OUT, step)
     first_z(IN)
     from_x(OUT, 1)
-    multiply(OUT, 0, 1)
+    multiply(OUT, 1, 1)
     from_x(OUT, 2)
     multiply(OUT, 2, 2)
     for step in range(3, n_z):
         from_x(OUT, step)
     send_x(IN, 0)
     multiply(OUT, 3, n_z)
-    squares[d, m] = (acc[...] * acc[...]).astype(jnp.bfloat16)
+    squares[m, pl.ds(pl.multiple_of(d * tok, tok), tok)] = (acc[...] * acc[...]).astype(jnp.bfloat16)
 
     first_z(SQ)
     send_x(SQ, 0)
@@ -328,6 +327,9 @@
     from_x(IN, 0)
     from_x(SQ, 0)
     send_x(IN, 1)
+    for one in load_basis(basis_in):
+        one.wait()
+    multiply(IN, 0, 0)
     for step in range(2, n_z):
         along_z(SQ, step)
         along_z(IN, step)
@@ -344,13 +346,13 @@
                 start(True, lambda h=h: d_copy(h))
     pairs(IN, n_z - 1)
     pairs(SQ, n_z - 1)
-    for one in load_basis(basis_in):
-        one.wait()
     from_x(IN, 1)
-    multiply(IN, 0, 1)
-    for step in range(2, n_z):
+    multiply(IN, 1, 1)
+    from_x(IN, 2)
+    multiply(IN, 2, 2)
+    for step in range(3, n_z):
         from_x(IN, step)
-    multiply(IN, 2, n_z)
+    multiply(IN, 3, n_z)
     for k in range(n_dp):
         piece = acc[:, k * rows:(k + 1) * rows]
         sq_in_send[k] = (piece * piece).T.astype(jnp.bfloat16)
@@ -370,11 +372,11 @@
         back = (d + n_dp - k - 1) % n_dp
         remote(grads.at[back], gsend.at[k], grecv.at[k], {"dp": others[k]}).wait_recv()
         remote(sq_in.at[back], isend.at[k], irecv.at[k], {"dp": others[k]}).wait_recv()
-    from_core(0)
-    from_core(1)
-    finish(0, 1)
-    for step in range(2, n_z):
-        from_y(step)
+    for k in range(n_dp):
+        sq_all[:, k * tok:(k + 1) * tok] = sq_in[k]
+    for step in range(n_z):
+        if step > 1:
+            from_y(step)
         from_core(step)
         finish(step, step)
 
@@ -400,9 +402,10 @@
         out_specs=spec,
         scratch_shapes=[
             pltpu.VMEM((2, n_mp, tok, feat), jnp.bfloat16),
-            pltpu.VMEM((n_dp, n_mp, tok, cols), jnp.bfloat16),
+            pltpu.VMEM((n_mp, n_dp * tok, cols), jnp.bfloat16),
             pltpu.VMEM((n_dp, rows, tok), jnp.bfloat16),
             pltpu.VMEM((n_dp, rows, tok), jnp.bfloat16),
+            pltpu.VMEM((rows, n_dp * tok), jnp.bfloat16),
             pltpu.VMEM((n_dp, rows, width), jnp.bfloat16),
             pltpu.VMEM((n_mp, feat, cols), jnp.bfloat16),
             pltpu.VMEM((tok, cols), jnp.float32),

time: 174 us -> 173 us (level)
  no operation moved by 1% of the time
where the time goes in v3:
time: 173 us
  Pallas kernels  168 us (97%)
  local copies, waits for them, and re-layouts  4.64 us (3%)
    pallas_call x1, Pallas kernels, per_device(): pl.pallas_call(kernel, out_shape=jax.ShapeDtypeStruct((rows, depth), jnp....  168 us
    unnamed x1, local copies, waits for them, and re-layouts  4.64 us

profile of v3, /device:TPU:0, one launch (start us, length us, event | category | flops | bytes accessed | tf_op | source)
XLA Modules:
  0.0 173.1 jit_solution(1796730851551201634)
XLA Ops:
  0.0 168.5 %shard_map.55 = bf16[256,8192]{1,0:T(8,128)(2,1)} custom-call(bf16[256,1024]{1,0:T(8,128)(2,1)} %act.1, bf16[256,1024]{1,0:T(8,128)(2,1)} %og.1, bf16[8192,1024]{1,0:T(8,128)(2,1)} %basis_in.1, bf16[8192,1024]{1,0:T(8,128)(2,1)} %basis_out.1, bf16[1024,2048]{1,0:T(8,128)(2,1)} %grad.1), custom_call_target="tpu_custom_call" | custom-call | flops 12884901888 | bytes 41943040 | tf_op jit(solution)/shard_map/pallas_call | solution.py:398
  168.5 4.6 %copy.7 = bf16[256,8192]{1,0:T(8,128)(2,1)} copy(bf16[256,8192]{1,0:T(8,128)(2,1)} %shard_map.55) | data formatting | bytes 8388608

commit v4 on v3

--- a/solution.py
+++ b/solution.py
@@ -39,20 +39,18 @@
 def kernel(
     act, og, basis_in, basis_out, grad, out,
     held, squares, sq_in, sq_in_send, sq_all, grads, basis, acc, result,
-    load_sem, store_sem, zsend, zrecv, xsend, xrecv, dsend, drecv, ysend, yrecv, csend, crecv,
-    gsend, grecv, isend, irecv,
+    load_sem, store_sem, zsend, zrecv, xsend, xrecv, dsend, drecv, ysend, yrecv, own_send, own_recv,
+    gsend, grecv, isend, irecv, rsend, rrecv,
 ):
     tok, feat = act.shape
     n_mp, n_dp = held.shape[1], sq_in.shape[0]
     n_z = n_mp // 2
     rows = out.shape[0]
-    width = grad.shape[1]
     half = tok // 2
     d, m = lax.axis_index("dp"), lax.axis_index("mp")
     y, c = d // 2, d % 2
     z, x = m // 2, m % 2
     y_peer, c_peer, x_peer = (1 - y) * 2 + c, y * 2 + 1 - c, z * 2 + 1 - x
-    diagonal = (1 - y) * 2 + 1 - c
     others = [(d + i) % n_dp for i in range(1, n_dp)]
     started = []
 
@@ -78,10 +76,14 @@
         at = z - step if way == UP else z + step
         return at * 2 + ((1 - x) if other_x else x)
 
-    def there(step, way):
+    def mine(step):
+        return (z + step) % 2 == c
+
+    def there(a, step, way):
         if step == 0:
-            return True
-        return z >= step if way == UP else z + step < n_z
+            return mine(0) if a == SQ else True
+        near = z >= step if way == UP else z + step < n_z
+        return near & mine(step) if a == SQ else near
 
     def ways(step):
         return (UP,) if step == 0 else (UP, DOWN)
@@ -89,21 +91,19 @@
     def can_pass(way):
         return z < n_z - 1 if way == UP else z > 0
 
-    def paired(step, way, h):
+    def paired(a, step, way):
+        return there(a, step, way) & (z == step if way == UP else z + step == n_z - 1)
+
+    def alone(a, step, way, h):
         if h == 0 or step == 0:
-            return False
-        return z == step if way == UP else z + step == n_z - 1
-
-    def alone(step, way, h):
-        if h == 0 or step == 0:
-            return there(step, way)
-        return z > step if way == UP else z + step < n_z - 1
+            return there(a, step, way)
+        return there(a, step, way) & (z > step if way == UP else z + step < n_z - 1)
 
     def part(a, step, way, other_x, h, owner=None):
         slot = slot_of(step, way, other_x)
         if a == SQ:
-            lines = (d if owner is None else owner) * tok + h * half
-            return squares.at[slot, pl.ds(pl.multiple_of(lines, half), half)]
+            lines = ((y if owner is None else owner) * 2 + h) * tok
+            return squares.at[slot, pl.ds(pl.multiple_of(lines, tok), tok)]
         return held.at[a, slot, pl.ds(h * half, half)]
 
     def remote(ref, send, recv, target):
@@ -122,15 +122,19 @@
         return remote(part(a, step, way, other_x, h), xsend.at[at], xrecv.at[at], {"mp": x_peer})
 
     def d_copy(h, other_x=0):
-        return remote(part(SQ, 0, UP, other_x, h, y_peer), dsend.at[h], drecv.at[h], {"mp": x_peer})
+        return remote(part(SQ, 0, UP, other_x, h, 1 - y), dsend.at[h], drecv.at[h], {"mp": x_peer})
 
     def y_copy(step, way, other_x, h, owner):
         at = (step, way, other_x, h)
         return remote(part(SQ, *at, owner), ysend.at[at], yrecv.at[at], {"dp": y_peer})
 
-    def c_copy(step, way, other_x, h, far, owner):
-        at = (step, way, other_x, h)
-        return remote(part(SQ, *at, owner), csend.at[(far,) + at], crecv.at[(far,) + at], {"dp": c_peer})
+    def own_copy():
+        lines = pl.ds(pl.multiple_of(d * tok, tok), tok)
+        return remote(squares.at[m, lines], own_send, own_recv, {"dp": c_peer})
+
+    def own_copy_in():
+        lines = pl.ds(pl.multiple_of(c_peer * tok, tok), tok)
+        return remote(squares.at[m, lines], own_send, own_recv, {"dp": c_peer})
 
     def send_z(a, step, way, other_x, h, wanted):
         if step < n_z - 1:
@@ -139,22 +143,33 @@
     def send_x(a, step):
         for h in (0, 1):
             for way in ways(step):
-                start(alone(step, way, h), lambda way=way, h=h: x_copy(a, step, way, h))
+                start(alone(a, step, way, h), lambda way=way, h=h: x_copy(a, step, way, h))
 
     def spread(step, way, other_x, h, wanted):
         if step > 0 or not other_x:
-            start(wanted, lambda: y_copy(step, way, other_x, h, d))
-        start(wanted, lambda: c_copy(step, way, other_x, h, 0, d))
+            start(wanted, lambda: y_copy(step, way, other_x, h, y))
 
     def first_z(a):
         for h in (0, 1):
             for way in (UP, DOWN):
                 send_z(a, 0, way, 0, h, True)
 
+    def first_squares():
+        start((z % 2) != c, own_copy)
+        for own in (True, False):
+            if not own:
+                arrived(mine(0), own_copy_in)
+            for h in (0, 1):
+                wanted = mine(0) & (c == h if own else c != h)
+                for way in (UP, DOWN):
+                    send_z(SQ, 0, way, 0, h, wanted)
+                spread(0, UP, 0, h, wanted)
+                start(wanted, lambda h=h: x_copy(SQ, 0, UP, h))
+
     def along_z(a, step):
         for h in (0, 1):
             for way in (UP, DOWN):
-                wanted = there(step, way)
+                wanted = there(a, step, way)
                 arrived(wanted, lambda: z_copy_in(a, step, way, 0, h))
                 send_z(a, step, way, 0, h, wanted)
                 if a == SQ:
@@ -167,7 +182,7 @@
 
     def pairs(a, step):
         for way in (UP, DOWN):
-            wanted = paired(step, way, 1)
+            wanted = paired(a, step, way)
             arrived(wanted, lambda: z_copy_in(a, step, way, 1, 1))
             send_z(a, step, way, 1, 1, wanted)
             if a == SQ:
@@ -176,11 +191,11 @@
     def from_x(a, step):
         for h in (0, 1):
             for way in ways(step):
-                wanted = alone(step, way, h)
+                wanted = alone(a, step, way, h)
                 arrived(wanted, lambda: x_copy(a, step, way, h, 1))
                 if step == 0 and h == 1:
-                    send_z(a, 0, UP, 1, h, z == 0)
-                    send_z(a, 0, DOWN, 1, h, z == n_z - 1)
+                    send_z(a, 0, UP, 1, h, both(wanted, z == 0))
+                    send_z(a, 0, DOWN, 1, h, both(wanted, z == n_z - 1))
                 if a == SQ:
                     spread(step, way, 1, h, wanted)
 
@@ -188,17 +203,7 @@
         for other_x in (0, 1) if step > 0 else (0,):
             for h in (0, 1):
                 for way in ways(step):
-                    wanted = there(step, way)
-                    arrived(wanted, lambda: y_copy(step, way, other_x, h, y_peer))
-                    start(wanted, lambda way=way, other_x=other_x, h=h: c_copy(step, way, other_x, h, 1, y_peer))
-
-    def from_core(step):
-        for other_x in (0, 1):
-            for h in (0, 1):
-                for way in ways(step):
-                    wanted = there(step, way)
-                    arrived(wanted, lambda: c_copy(step, way, other_x, h, 0, c_peer))
-                    arrived(wanted, lambda: c_copy(step, way, other_x, h, 1, diagonal))
+                    arrived(there(SQ, step, way), lambda: y_copy(step, way, other_x, h, 1 - y))
 
     def load_basis(source):
         return [
@@ -225,32 +230,46 @@
 
         blocks_within(low, high, block)
 
+    def place(i):
+        return (i // 4) * 2 + i % 2
+
+    def columns_of(i):
+        return pl.ds(pl.multiple_of(i * feat, feat), feat)
+
     def store(i):
-        cols = pl.ds(pl.multiple_of(i * feat, feat), feat)
-        return pltpu.make_async_copy(result.at[:, cols], out.at[:, cols], store_sem.at[i])
+        mine_rows = pl.ds(pl.multiple_of(c * rows, rows), rows)
+        return pltpu.make_async_copy(result.at[place(i), mine_rows], out.at[:, columns_of(i)], store_sem.at[place(i)])
+
+    def hand_over(i):
+        their_rows = pl.ds(pl.multiple_of((1 - c) * rows, rows), rows)
+        return pltpu.make_async_remote_copy(
+            src_ref=result.at[place(i), their_rows], dst_ref=out.at[:, columns_of(i)],
+            send_sem=rsend.at[place(i)], recv_sem=rrecv.at[place(i)],
+            device_id={"dp": c_peer}, device_id_type=MESH,
+        )
 
     def finish(low, high):
-        per_grad = width // feat
-
         def block(i):
-            @pl.loop(0, feat // tile)
-            def _(j):
-                cols = pl.ds(pl.multiple_of(j * tile, tile), tile)
-                total = jnp.dot(sq_all[...], squares[i, :, cols], preferred_element_type=jnp.float32)
-                scaling = total / (tok * n_dp)
-                at_grad = pl.ds(pl.multiple_of((i % per_grad) * feat + j * tile, tile), tile)
-                top = grads[i // per_grad, :, at_grad].astype(jnp.float32)
-                at_out = pl.ds(pl.multiple_of(i * feat + j * tile, tile), tile)
-                result[:, at_out] = (top / (scaling + damping)).astype(result.dtype)
-
-            store(i).start()
+            @pl.when((i // 2) % 2 == c)
+            def _():
+                @pl.loop(0, feat // tile)
+                def _(j):
+                    cols = pl.ds(pl.multiple_of(j * tile, tile), tile)
+                    total = jnp.dot(sq_all[...], squares[i, :, cols], preferred_element_type=jnp.float32)
+                    scaling = total / (tok * n_dp)
+                    at_grad = pl.ds(pl.multiple_of((i % 2) * feat + j * tile, tile), tile)
+                    top = grads[i // 4, :, at_grad].astype(jnp.float32)
+                    result[place(i), :, cols] = (top / (scaling + damping)).astype(result.dtype)
+
+                hand_over(i).start()
+                store(i).start()
 
         blocks_within(low, high, block)
 
     own_out = pltpu.make_async_copy(og, held.at[OUT, m], load_sem.at[n_mp])
     own_in = pltpu.make_async_copy(act, held.at[IN, m], load_sem.at[n_mp + 1])
     own_grad = pltpu.make_async_copy(
-        grad.at[pl.ds(pl.multiple_of(d * rows, rows), rows), :], grads.at[d], load_sem.at[n_mp + 2]
+        grad.at[pl.ds(pl.multiple_of(y * 2 * rows, 2 * rows), 2 * rows), :], grads.at[y], load_sem.at[n_mp + 2]
     )
     own_out.start()
     own_in.start()
@@ -270,16 +289,16 @@
     inner = (z > 0).astype(jnp.int32) + (z < n_z - 1).astype(jnp.int32)
     pl.semaphore_wait(barrier, len(peers) + inner)
 
-    def grad_copy(k, other):
+    def grad_copy():
         return pltpu.make_async_remote_copy(
-            src_ref=grad.at[pl.ds(pl.multiple_of(other * rows, rows), rows), :], dst_ref=grads.at[d],
-            send_sem=gsend.at[k], recv_sem=grecv.at[k],
-            device_id={"dp": other}, device_id_type=MESH,
+            src_ref=grad.at[pl.ds(pl.multiple_of((1 - y) * 2 * rows, 2 * rows), 2 * rows), :], dst_ref=grads.at[y],
+            send_sem=gsend, recv_sem=grecv,
+            device_id={"dp": y_peer}, device_id_type=MESH,
         )
 
     def in_copy(k, other):
         return pltpu.make_async_remote_copy(
-            src_ref=sq_in_send.at[other], dst_ref=sq_in.at[d],
+            src_ref=sq_in_send.at[other // 2], dst_ref=sq_in.at[d],
             send_sem=isend.at[k], recv_sem=irecv.at[k],
             device_id={"dp": other}, device_id_type=MESH,
         )
@@ -287,8 +306,7 @@
     own_out.wait()
     first_z(OUT)
     send_x(OUT, 0)
-    for k, other in enumerate(others):
-        start(True, lambda k=k, other=other: grad_copy(k, other))
+    start(True, grad_copy)
     own_in.wait()
     along_z(OUT, 1)
     send_x(OUT, 1)
@@ -313,10 +331,7 @@
     multiply(OUT, 3, n_z)
     squares[m, pl.ds(pl.multiple_of(d * tok, tok), tok)] = (acc[...] * acc[...]).astype(jnp.bfloat16)
 
-    first_z(SQ)
-    send_x(SQ, 0)
-    for h in (0, 1):
-        spread(0, UP, 0, h, True)
+    first_squares()
     for one in load_basis(basis_in):
         one.start()
     acc[...] = jnp.zeros_like(acc)
@@ -343,7 +358,7 @@
         send_x(SQ, step)
         if step == 2:
             for h in (0, 1):
-                start(True, lambda h=h: d_copy(h))
+                start(mine(0), lambda h=h: d_copy(h))
     pairs(IN, n_z - 1)
     pairs(SQ, n_z - 1)
     from_x(IN, 1)
@@ -353,35 +368,36 @@
     for step in range(3, n_z):
         from_x(IN, step)
     multiply(IN, 3, n_z)
-    for k in range(n_dp):
-        piece = acc[:, k * rows:(k + 1) * rows]
+    for k in range(2):
+        piece = acc[:, k * 2 * rows:(k + 1) * 2 * rows]
         sq_in_send[k] = (piece * piece).T.astype(jnp.bfloat16)
     for k, other in enumerate(others):
         start(True, lambda k=k, other=other: in_copy(k, other))
-    sq_in[d] = sq_in_send[d]
+    sq_in[d] = sq_in_send[y]
     from_x(SQ, 2)
     from_y(1)
     for h in (0, 1):
-        arrived(True, lambda: d_copy(h, 1))
-        start(True, lambda h=h: c_copy(0, UP, 1, h, 1, y_peer))
+        arrived(mine(0), lambda: d_copy(h, 1))
     for step in range(3, n_z):
         from_x(SQ, step)
 
     own_grad.wait()
+    remote(grads.at[1 - y], gsend, grecv, {"dp": y_peer}).wait_recv()
     for k in range(n_dp - 1):
         back = (d + n_dp - k - 1) % n_dp
-        remote(grads.at[back], gsend.at[k], grecv.at[k], {"dp": others[k]}).wait_recv()
         remote(sq_in.at[back], isend.at[k], irecv.at[k], {"dp": others[k]}).wait_recv()
     for k in range(n_dp):
         sq_all[:, k * tok:(k + 1) * tok] = sq_in[k]
     for step in range(n_z):
         if step > 1:
             from_y(step)
-        from_core(step)
         finish(step, step)
 
-    for i in range(n_mp):
+    for k in range(n_mp // 2):
+        i = (k // 2) * 4 + c * 2 + k % 2
         store(i).wait()
+        hand_over(i).wait_send()
+        hand_over((k // 2) * 4 + (1 - c) * 2 + k % 2).wait_recv()
     for wanted, copy in started:
         do(wanted, lambda: copy().wait_send())
 
@@ -403,21 +419,22 @@
         scratch_shapes=[
             pltpu.VMEM((2, n_mp, tok, feat), jnp.bfloat16),
             pltpu.VMEM((n_mp, n_dp * tok, cols), jnp.bfloat16),
-            pltpu.VMEM((n_dp, rows, tok), jnp.bfloat16),
-            pltpu.VMEM((n_dp, rows, tok), jnp.bfloat16),
-            pltpu.VMEM((rows, n_dp * tok), jnp.bfloat16),
-            pltpu.VMEM((n_dp, rows, width), jnp.bfloat16),
+            pltpu.VMEM((n_dp, 2 * rows, tok), jnp.bfloat16),
+            pltpu.VMEM((2, 2 * rows, tok), jnp.bfloat16),
+            pltpu.VMEM((2 * rows, n_dp * tok), jnp.bfloat16),
+            pltpu.VMEM((2, 2 * rows, width), jnp.bfloat16),
             pltpu.VMEM((n_mp, feat, cols), jnp.bfloat16),
             pltpu.VMEM((tok, cols), jnp.float32),
-            pltpu.VMEM((rows, depth), jnp.bfloat16),
-            dma((n_mp + 3,)), dma((n_mp,)),
+            pltpu.VMEM((n_mp // 2, 2 * rows, feat), jnp.bfloat16),
+            dma((n_mp + 3,)), dma((n_mp // 2,)),
             dma((3, n_z - 1, 2, 2, 2)), dma((3, n_z - 1, 2, 2, 2)),
             dma((3, n_z, 2, 2)), dma((3, n_z, 2, 2)),
             dma((2,)), dma((2,)),
             dma((n_z, 2, 2, 2)), dma((n_z, 2, 2, 2)),
-            dma((2, n_z, 2, 2, 2)), dma((2, n_z, 2, 2, 2)),
+            dma, dma,
+            dma, dma,
             dma((n_dp,)), dma((n_dp,)),
-            dma((n_dp,)), dma((n_dp,)),
+            dma((n_mp // 2,)), dma((n_mp // 2,)),
         ],
         compiler_params=pltpu.CompilerParams(
             collective_id=0, has_side_effects=True, vmem_limit_bytes=60 * 1024 * 1024

time: 173 us -> 173 us (level)
  no operation moved by 1% of the time
where the time goes in v4:
time: 173 us
  Pallas kernels  168 us (97%)
  local copies, waits for them, and re-layouts  4.64 us (3%)
    pallas_call x1, Pallas kernels, per_device(): pl.pallas_call(kernel, out_shape=jax.ShapeDtypeStruct((rows, depth), jnp....  168 us
    unnamed x1, local copies, waits for them, and re-layouts  4.64 us

profile of v4, /device:TPU:0, one launch (start us, length us, event | category | flops | bytes accessed | tf_op | source)
XLA Modules:
  0.0 172.6 jit_solution(10642900511616433993)
XLA Ops:
  0.0 168.0 %shard_map.55 = bf16[256,8192]{1,0:T(8,128)(2,1)} custom-call(bf16[256,1024]{1,0:T(8,128)(2,1)} %act.1, bf16[256,1024]{1,0:T(8,128)(2,1)} %og.1, bf16[8192,1024]{1,0:T(8,128)(2,1)} %basis_in.1, bf16[8192,1024]{1,0:T(8,128)(2,1)} %basis_out.1, bf16[1024,2048]{1,0:T(8,128)(2,1)} %grad.1), custom_call_target="tpu_custom_call" | custom-call | flops 12884901888 | bytes 41943040 | tf_op jit(solution)/shard_map/pallas_call | solution.py:414
  168.0 4.6 %copy.7 = bf16[256,8192]{1,0:T(8,128)(2,1)} copy(bf16[256,8192]{1,0:T(8,128)(2,1)} %shard_map.55) | data formatting | bytes 8388608

commit v5 on v4

--- a/solution.py
+++ b/solution.py
@@ -296,12 +296,17 @@
             device_id={"dp": y_peer}, device_id_type=MESH,
         )
 
-    def in_copy(k, other):
+    def in_copy(k):
+        src = (sq_in_send.at[1 - y], sq_in_send.at[y], sq_in.at[y_peer])[k]
+        dst = (sq_in.at[d], sq_in.at[d], sq_in.at[y_peer])[k]
         return pltpu.make_async_remote_copy(
-            src_ref=sq_in_send.at[other // 2], dst_ref=sq_in.at[d],
-            send_sem=isend.at[k], recv_sem=irecv.at[k],
-            device_id={"dp": other}, device_id_type=MESH,
+            src_ref=src, dst_ref=dst, send_sem=isend.at[k], recv_sem=irecv.at[k],
+            device_id={"dp": (y_peer, c_peer, c_peer)[k]}, device_id_type=MESH,
         )
+
+    def in_copy_in(k):
+        owner = (y_peer, c_peer, (1 - y) * 2 + 1 - c)[k]
+        return remote(sq_in.at[owner], isend.at[k], irecv.at[k], {"dp": c_peer})
 
     own_out.wait()
     first_z(OUT)
@@ -356,9 +361,8 @@
             from_y(0)
     for step in range(2, n_z):
         send_x(SQ, step)
-        if step == 2:
-            for h in (0, 1):
-                start(mine(0), lambda h=h: d_copy(h))
+    for h in (0, 1):
+        start(mine(0), lambda h=h: d_copy(h))
     pairs(IN, n_z - 1)
     pairs(SQ, n_z - 1)
     from_x(IN, 1)
@@ -371,27 +375,26 @@
     for k in range(2):
         piece = acc[:, k * 2 * rows:(k + 1) * 2 * rows]
         sq_in_send[k] = (piece * piece).T.astype(jnp.bfloat16)
-    for k, other in enumerate(others):
-        start(True, lambda k=k, other=other: in_copy(k, other))
+    start(True, lambda: in_copy(0))
+    start(True, lambda: in_copy(1))
     sq_in[d] = sq_in_send[y]
-    from_x(SQ, 2)
-    from_y(1)
+    for step in range(2, n_z):
+        from_x(SQ, step)
+    arrived(True, lambda: in_copy_in(0))
+    start(True, lambda: in_copy(2))
+
+    own_grad.wait()
+    remote(grads.at[1 - y], gsend, grecv, {"dp": y_peer}).wait_recv()
+    arrived(True, lambda: in_copy_in(1))
+    arrived(True, lambda: in_copy_in(2))
+    for k in range(n_dp):
+        sq_all[:, k * tok:(k + 1) * tok] = sq_in[k]
+    for step in range(1, n_z):
+        from_y(step)
+        finish(step, step)
     for h in (0, 1):
         arrived(mine(0), lambda: d_copy(h, 1))
-    for step in range(3, n_z):
-        from_x(SQ, step)
-
-    own_grad.wait()
-    remote(grads.at[1 - y], gsend, grecv, {"dp": y_peer}).wait_recv()
-    for k in range(n_dp - 1):
-        back = (d + n_dp - k - 1) % n_dp
-        remote(sq_in.at[back], isend.at[k], irecv.at[k], {"dp": others[k]}).wait_recv()
-    for k in range(n_dp):
-        sq_all[:, k * tok:(k + 1) * tok] = sq_in[k]
-    for step in range(n_z):
-        if step > 1:
-            from_y(step)
-        finish(step, step)
+    finish(0, 0)
 
     for k in range(n_mp // 2):
         i = (k // 2) * 4 + c * 2 + k % 2

time: 173 us -> 171 us (0.988)
  Pallas kernels: 168 us -> 166 us
where the time goes in v5:
time: 171 us
  Pallas kernels  166 us (97%)
  local copies, waits for them, and re-layouts  4.64 us (3%)
    pallas_call x1, Pallas kernels, per_device(): pl.pallas_call(kernel, out_shape=jax.ShapeDtypeStruct((rows, depth), jnp....  166 us
    unnamed x1, local copies, waits for them, and re-layouts  4.64 us

profile of v5, /device:TPU:0, one launch (start us, length us, event | category | flops | bytes accessed | tf_op | source)
XLA Modules:
  0.0 171.0 jit_solution(8724710111650187877)
XLA Ops:
  0.0 166.4 %shard_map.55 = bf16[256,8192]{1,0:T(8,128)(2,1)} custom-call(bf16[256,1024]{1,0:T(8,128)(2,1)} %act.1, bf16[256,1024]{1,0:T(8,128)(2,1)} %og.1, bf16[8192,1024]{1,0:T(8,128)(2,1)} %basis_in.1, bf16[8192,1024]{1,0:T(8,128)(2,1)} %basis_out.1, bf16[1024,2048]{1,0:T(8,128)(2,1)} %grad.1), custom_call_target="tpu_custom_call" | custom-call | flops 12884901888 | bytes 41943040 | tf_op jit(solution)/shard_map/pallas_call | solution.py:417
  166.4 4.6 %copy.7 = bf16[256,8192]{1,0:T(8,128)(2,1)} copy(bf16[256,8192]{1,0:T(8,128)(2,1)} %shard_map.55) | data formatting | bytes 8388608

commit v6 on v5

--- a/solution.py
+++ b/solution.py
@@ -352,17 +352,16 @@
     multiply(IN, 0, 0)
     for step in range(2, n_z):
         along_z(SQ, step)
+        send_x(SQ, step)
         along_z(IN, step)
         send_x(IN, step)
+        from_x(SQ, step - 1)
+        if step == 2:
+            from_y(0)
+            for h in (0, 1):
+                start(mine(0), lambda h=h: d_copy(h))
         pairs(IN, step - 1)
         pairs(SQ, step - 1)
-        if step == 2:
-            from_x(SQ, 1)
-            from_y(0)
-    for step in range(2, n_z):
-        send_x(SQ, step)
-    for h in (0, 1):
-        start(mine(0), lambda h=h: d_copy(h))
     pairs(IN, n_z - 1)
     pairs(SQ, n_z - 1)
     from_x(IN, 1)
@@ -378,8 +377,7 @@
     start(True, lambda: in_copy(0))
     start(True, lambda: in_copy(1))
     sq_in[d] = sq_in_send[y]
-    for step in range(2, n_z):
-        from_x(SQ, step)
+    from_x(SQ, n_z - 1)
     arrived(True, lambda: in_copy_in(0))
     start(True, lambda: in_copy(2))
 

time: 171 us -> 170 us (level)
  Pallas kernels: 166 us -> 164 us
    pallas_call x1, Pallas kernels: 166 us -> 164 us  [per_device(): pl.pallas_call(kernel, out_shape=jax.ShapeDtypeStruct((rows, depth), jnp....]
where the time goes in v6:
time: 170 us; the launch traced here: 169 us
  Pallas kernels  164 us (96%)
  local copies, waits for them, and re-layouts  4.64 us (3%)
    pallas_call x1, Pallas kernels, per_device(): pl.pallas_call(kernel, out_shape=jax.ShapeDtypeStruct((rows, depth), jnp....  164 us
    unnamed x1, local copies, waits for them, and re-layouts  4.64 us

profile of v6, /device:TPU:0, one launch (start us, length us, event | category | flops | bytes accessed | tf_op | source)
XLA Modules:
  0.0 168.6 jit_solution(14468169778698619171)
XLA Ops:
  0.0 164.0 %shard_map.55 = bf16[256,8192]{1,0:T(8,128)(2,1)} custom-call(bf16[256,1024]{1,0:T(8,128)(2,1)} %act.1, bf16[256,1024]{1,0:T(8,128)(2,1)} %og.1, bf16[8192,1024]{1,0:T(8,128)(2,1)} %basis_in.1, bf16[8192,1024]{1,0:T(8,128)(2,1)} %basis_out.1, bf16[1024,2048]{1,0:T(8,128)(2,1)} %grad.1), custom_call_target="tpu_custom_call" | custom-call | flops 12884901888 | bytes 41943040 | tf_op jit(solution)/shard_map/pallas_call | solution.py:415
  164.0 4.6 %copy.7 = bf16[256,8192]{1,0:T(8,128)(2,1)} copy(bf16[256,8192]{1,0:T(8,128)(2,1)} %shard_map.55) | data formatting | bytes 8388608
